TPU v7x, 32 devices: a whole 2x2x4 slice. The times are simulated.
32 devices in a mesh: groups: 2 (over x), dp: 16 (over z, y, core).
Axes of the slice: x: 2, y: 2, z: 4, core: 2. Of those that a mesh axis runs over, the one named last changes fastest.
Arguments:
- tokens: bfloat16 [8192, 8192], P(('groups', 'dp')), parts along dimension 0, may hold values from -6 to 6
- cotangent: bfloat16 [8192, 512], P(('groups', 'dp')), parts along dimension 0, may hold values from -1.5 to 1.5
- frozen_weight: bfloat16 [8192, 512], P('dp'), may hold values from -4 to 4
- frozen_scale: float32 [1], replicated, may hold values from 0.006 to 0.02
- adapter_down_weight: bfloat16 [128, 8192, 16], P('groups', 'dp'), parts along dimension 0, may hold values from -0.0625 to 0.0625
- adapter_up_weight: bfloat16 [128, 16, 512], P('groups'), parts along dimension 0, may hold values from -1.5 to 1.5
- sequence_adapter: int32 [64], P(('groups', 'dp')), parts along dimension 0, may hold values from 0 to 63
- sequence_token_length: int32 [64], P(('groups', 'dp')), parts along dimension 0, may hold values from 1 to 128, 2048 in all
Outputs:
- projection_output: bfloat16 [8192, 512], P(('groups', 'dp')), parts along dimension 0
- token_input_gradient: bfloat16 [8192, 8192], P(('groups', 'dp')), parts along dimension 0
- down_grad: float32 [128, 8192, 16], P('groups', 'dp'), parts along dimension 0
- adapter_up_gradient: float32 [128, 16, 512], P('groups', None, 'dp'), parts along dimension 0
There are 2 independent parts, one for each index of `groups`. A program takes and returns all parts, laid end to end along the dimension named above; an argument that names none is the same for every part. Nothing has to cross between parts.
Inputs may be any that keep to these rules, and one draw needn't show every extreme that they name: `sequence_token_length`: within each independent job (one group), the 32 lengths sum to 2048 and the largest equals 128.
All inputs are finite; a program needn't handle non-finite values.
Results may differ from a plain program's by a relative error of at most 0.001.
The roundings to bfloat16 on the way count: a program that leaves them out, or rounds other values in their place, can miss the bound.
Values may be sent and summed in bfloat16 or wider, within the bound.
A program may use at most 128 MiB of HBM per device.

v0:
```python
import jax
import jax.numpy as jnp
from jax import lax
from jax.sharding import PartitionSpec as P

adapter_scale = 2.0


def local(
    tokens,
    cotangent,
    frozen_weight,
    frozen_scale,
    adapter_down_weight,
    adapter_up_weight,
    sequence_adapter,
    sequence_token_length,
):
    tok_count, width = tokens.shape
    sequence_number = sequence_adapter.shape[0]
    slot_token_count = tok_count // sequence_number
    number_of_adapters, shard_width, adapter_rank_size = adapter_down_weight.shape
    output_width = frozen_weight.shape[1]
    scaling_factor = frozen_scale[0]
    every_adapter_index = lax.all_gather(sequence_adapter, "dp", axis=0, tiled=True)
    overall_sequences = every_adapter_index.shape[0]
    positions = lax.broadcasted_iota(jnp.int32, (sequence_number, slot_token_count), 1)
    valid_token_mask = (positions < sequence_token_length[:, None])[:, :, None]
    selected_down_weight = adapter_down_weight[every_adapter_index]
    adapter_range = jnp.arange(number_of_adapters, dtype=jnp.int32)[:, None]
    select_all = (every_adapter_index[None, :] == adapter_range).astype(jnp.float32)
    columns = lax.all_to_all(tokens, "dp", split_axis=1, concat_axis=0, tiled=True)
    columns_seq = columns.reshape(overall_sequences, slot_token_count, shard_width)
    term = jnp.einsum(
        "spc,scr->spr", columns_seq, selected_down_weight, preferred_element_type=jnp.float32
    )
    rank_sum = lax.psum_scatter(
        term.reshape(sequence_number * lax.axis_size("dp"), slot_token_count * adapter_rank_size),
        "dp",
        scatter_dimension=0,
        tiled=True,
    )
    rank_activations_rows = rank_sum.reshape(
        sequence_number, slot_token_count, adapter_rank_size
    ).astype(jnp.bfloat16)
    selected_up_weight = adapter_up_weight[sequence_adapter]
    adapter_output = jnp.einsum(
        "awl,ali->awi",
        rank_activations_rows,
        selected_up_weight,
        preferred_element_type=jnp.float32,
    )
    masked_cot = jnp.where(
        valid_token_mask,
        cotangent.reshape(sequence_number, slot_token_count, output_width),
        jnp.zeros((), jnp.bfloat16),
    )
    cot_flat = masked_cot.reshape(tok_count, output_width)
    frozen_output = jnp.dot(
        tokens,
        lax.all_gather(frozen_weight, "dp", axis=0, tiled=True),
        preferred_element_type=jnp.float32,
    )
    frozen_input_grad = lax.dot_general(
        cot_flat,
        lax.all_gather(frozen_weight, "dp", axis=0, tiled=True),
        (((1,), (1,)), ((), ())),
        preferred_element_type=jnp.float32,
    )
    combined_output = (
        scaling_factor * frozen_output.reshape(sequence_number, slot_token_count, output_width)
        + adapter_scale * adapter_output
    )
    projection_output = (
        jnp.where(valid_token_mask, combined_output, 0.0)
        .astype(jnp.bfloat16)
        .reshape(tok_count, output_width)
    )
    rank_gradient = (
        adapter_scale
        * jnp.einsum(
            "spo,sro->spr", masked_cot, selected_up_weight, preferred_element_type=jnp.float32
        )
    ).astype(jnp.bfloat16)
    per_sequence = jnp.einsum(
        "spr,spo->sro", rank_activations_rows, masked_cot, preferred_element_type=jnp.float32
    )
    select_local = (sequence_adapter[None, :] == adapter_range).astype(jnp.float32)
    partial_up_gradient = adapter_scale * jnp.dot(
        select_local,
        per_sequence.reshape(sequence_number, adapter_rank_size * output_width),
        precision=lax.Precision.HIGHEST,
    )
    adapter_up_gradient = lax.psum_scatter(
        partial_up_gradient.reshape(number_of_adapters, adapter_rank_size, output_width),
        "dp",
        scatter_dimension=2,
        tiled=True,
    )
    grad_flat = rank_gradient.reshape(sequence_number, slot_token_count * adapter_rank_size)
    grad_all = lax.all_gather(grad_flat, "dp", axis=0, tiled=True)
    grad_seq = grad_all.reshape(overall_sequences, slot_token_count, adapter_rank_size)
    down_terms = jnp.einsum(
        "spc,spr->scr", columns_seq, grad_seq, preferred_element_type=jnp.float32
    )
    adapter_columns = jnp.einsum(
        "spr,scr->spc", grad_seq, selected_down_weight, preferred_element_type=jnp.float32
    ).astype(jnp.bfloat16)
    adapter_input_grad = lax.all_to_all(
        adapter_columns.reshape(overall_sequences * slot_token_count, shard_width),
        "dp",
        split_axis=0,
        concat_axis=1,
        tiled=True,
    )
    down_grad = jnp.dot(
        select_all,
        down_terms.reshape(overall_sequences, shard_width * adapter_rank_size),
        precision=lax.Precision.HIGHEST,
    ).reshape(number_of_adapters, shard_width, adapter_rank_size)
    token_input_gradient = (
        scaling_factor * frozen_input_grad + adapter_input_grad.astype(jnp.float32)
    ).astype(jnp.bfloat16)
    return (projection_output, token_input_gradient, down_grad, adapter_up_gradient)


def solution(mesh):
    placed = (
        P(("groups", "dp"), None),
        P(("groups", "dp"), None),
        P("dp", None),
        P(),
        P("groups", "dp", None),
        P("groups", None, None),
        P(("groups", "dp")),
        P(("groups", "dp")),
    )
    return jax.shard_map(
        local,
        mesh=mesh,
        in_specs=placed,
        out_specs=(
            P(("groups", "dp"), None),
            P(("groups", "dp"), None),
            P("groups", "dp", None),
            P("groups", None, "dp"),
        ),
        check_vma=False,
    )
```

profile of v0, /device:TPU:5, one launch (start us, length us, event | category | flops | bytes accessed | tf_op | source)
XLA Modules:
  0.0 420.8 jit_solution(5205218451652262311)
XLA Ops:
  7.2 4.7 %copy.71 = bf16[32,16,8,512]{3,2,0,1:T(8,128)(2,1)} copy(bf16[32,16,8,512]{3,2,1,0:T(8,128)(2,1)} %bitcast.63) | data formatting | bytes 8388608 | tf_op jit(solution)/shard_map/all_to_all | solution.py:32
  11.9 6.8 %all-to-all-start = ((bf16[256,16,512]{2,0,1:T(8,128)(2,1)}), bf16[256,16,512]{2,0,1:T(8,128)(2,1)}, u32[]{:S(2)}, u32[]{:S(2)}) async-start(bf16[256,16,512]{2,0,1:T(8,128)(2,1)} %bitcast.59), calls=%async_computation | async-start | bytes 8388608 | tf_op jit(solution)/shard_map/all_to_all | solution.py:32
  18.8 0.7 all-gather.3.cloned.1.call-update
  19.5 1.8 gather_fusion.1
  21.4 0.2 fusion.5
  21.6 0.1 copy.46
  21.8 0.1 reshape.111
  21.9 148.4 %all-gather = bf16[16,2,2048]{2,1,0:T(2,128)(2,1)S(1)} all-gather(bf16[1,2,2048]{2,1,0:T(2,128)(2,1)S(1)} %reshape.111), channel_id=1, replica_groups=mesh['groups'=2,'dp'=16] {'dp'}, dimensions={0}, use_global_device_ids=true | all-gather | bytes 139264 | tf_op jit(solution)/shard_map/all_gather | solution.py:101
  170.3 0.7 reshape.85
  171.0 0.6 fusion.21
  172.3 0.2 dynamic-update-slice
  172.5 9.7 %all-reduce = s32[32]{0:T(128)S(1)} all-reduce(s32[32]{0:T(128)S(1)} %dynamic-update-slice), channel_id=1, replica_groups=mesh['groups'=2,'dp'=16] {'dp'}, use_global_device_ids=true, to_apply=%add | all-reduce | flops 32 | bytes 256
  182.3 0.6 gather_fusion
  182.9 3.1 convolution_convert_fusion
  186.0 7.6 %all-to-all-start.1 = ((bf16[16,256,512]{2,1,0:T(8,128)(2,1)}), bf16[16,256,512]{2,1,0:T(8,128)(2,1)}, u32[]{:S(2)}, u32[]{:S(2)}) async-start(bf16[16,256,512]{2,1,0:T(8,128)(2,1)} %bitcast.60), calls=%async_computation.1 | async-start | bytes 8388608 | tf_op jit(solution)/shard_map/all_to_all | solution.py:109
  194.9 3.4 convolution_bitcast_fusion.1
  198.3 0.6 copy.43
  198.9 132.4 %all-reduce.3 = bf16[32,2048]{0,1:T(8,128)(2,1)S(1)} all-reduce(f32[32,2048]{0,1:T(8,128)S(1)} %bitcast.62), channel_id=2, replica_groups=mesh['groups'=2,'dp'=16] {'dp'}, use_global_device_ids=true, to_apply=%region_0.0.clone | all-reduce | flops 65536 | bytes 393216
  331.3 0.2 dynamic-slice_convert_fusion
  331.5 0.9 copy.70
  332.5 0.3 convolution_bitcast_fusion.2
  332.8 2.3 convolution_multiply_fusion.1
  335.1 3.8 copy.60
  338.9 3.4 convert_bitcast_fusion
  342.3 4.3 %copy.64 = f32[16,32,8,512]{3,2,0,1:T(8,128)} copy(f32[16,32,8,512]{3,2,1,0:T(8,128)S(1)} %convert_bitcast_fusion) | data formatting | bytes 16777216 | tf_op jit(solution)/shard_map/convert_element_type | solution.py:122
  346.5 2.9 convolution_bitcast_fusion
  349.4 1.7 fusion.6
  351.1 2.5 copy.54
  353.7 7.7 %convolution_multiply_fusion.3 = f32[256,512]{1,0:T(8,128)S(1)} fusion(bf16[256,8192]{1,0:T(8,128)(2,1)} %param.8, bf16[8192,512]{1,0:T(8,128)(2,1)} %all-gather.3.cloned.1.call-done, f32[]{:T(128)} %bitcast.54), kind=kOutput, calls=%fused_computation.13 | convolution fusion | flops 2147614720 | bytes 13107204 | tf_op jit(solution)/shard_map/dot_general | solution.py:59
  361.4 0.9 fusion.4
  362.3 8.2 %fusion.1 = bf16[256,8192]{1,0:T(8,128)(2,1)} fusion(f32[256,8192]{1,0:T(8,128)S(1)} %bitcast.58, bf16[8192,512]{1,0:T(8,128)(2,1)} %all-gather.3.cloned.1.call-done, f32[]{:T(128)} %bitcast.55, bf16[256,512]{1,0:T(8,128)(2,1)S(1)} %copy-done.2, pred[256]{0:T(512)(128)(4,1)S(1)} %get-tuple-element.20), kind=kOutput, calls=%fused_computation.4 | convolution fusion | flops 2153906176 | bytes 21233924 | tf_op jit(solution)/shard_map/dot_general | solution.py:64
  370.6 43.4 %reduce-scatter.3.cloned.1.call-done = f32[64,16,32]{0,2,1:T(8,128)} async-done(((f32[64,16,512]{0,2,1:T(8,128)}), f32[64,16,32]{0,2,1:T(8,128)}) %reduce-scatter.3.cloned.1.call-update) | async-done | bytes 131088 | tf_op jit(solution)/shard_map/reduce_scatter | solution.py:94
  (30 shorter events, 0.3 us)
Async XLA Ops:
  7.2 175.1 %copy-start = (bf16[64,512,16]{1,2,0:T(8,128)(2,1)S(1)}, bf16[64,512,16]{1,2,0:T(8,128)(2,1)}, u32[]{:S(2)}) copy-start(bf16[64,512,16]{1,2,0:T(8,128)(2,1)} %param.12) | copy-start | bytes 3145732
  11.9 7.6 %copy-start.4 = (s32[2]{0:T(128)S(1)}, s32[2]{0:T(128)}, u32[]{:S(2)}) copy-start(s32[2]{0:T(128)} %param.14) | copy-start | bytes 28
  11.9 9.4 %copy-start.5 = (s32[2]{0:T(128)S(1)}, s32[2]{0:T(128)}, u32[]{:S(2)}) copy-start(s32[2]{0:T(128)} %param.15) | copy-start | bytes 28
  11.9 9.5 %copy-start.2 = (bf16[256,512]{1,0:T(8,128)(2,1)S(1)}, bf16[256,512]{1,0:T(8,128)(2,1)}, u32[]{:S(2)}) copy-start(bf16[256,512]{1,0:T(8,128)(2,1)} %param.9) | copy-start | bytes 786436
  11.9 159.1 %copy-start.3 = (u32[32]{0:T(128)S(1)}, u32[32]{0:T(128)}, u32[]{:S(2)}) copy-start(u32[32]{0:T(128)} %constant.18) | copy-start | bytes 388
  11.9 174.1 %all-to-all-start = ((bf16[256,16,512]{2,0,1:T(8,128)(2,1)}), bf16[256,16,512]{2,0,1:T(8,128)(2,1)}, u32[]{:S(2)}, u32[]{:S(2)}) async-start(bf16[256,16,512]{2,0,1:T(8,128)(2,1)} %bitcast.59), calls=%async_computation | async-start | bytes 8388608 | tf_op jit(solution)/shard_map/all_to_all | solution.py:32
  18.7 334.9 %all-gather.3.cloned.1.call-start = ((), (), s32[]{:S(2)}) async-start(), calls=%async_computation.3 | async-start | bytes 8912896 | tf_op jit(solution)/shard_map/all_gather | solution.py:61
  186.0 152.9 %all-to-all-start.1 = ((bf16[16,256,512]{2,1,0:T(8,128)(2,1)}), bf16[16,256,512]{2,1,0:T(8,128)(2,1)}, u32[]{:S(2)}, u32[]{:S(2)}) async-start(bf16[16,256,512]{2,1,0:T(8,128)(2,1)} %bitcast.60), calls=%async_computation.1 | async-start | bytes 8388608 | tf_op jit(solution)/shard_map/all_to_all | solution.py:109
  193.6 220.4 %reduce-scatter.3.cloned.1.call-start = ((), (), s32[]{:S(2)}) async-start(), calls=%async_computation.4 | async-start | bytes 4456448 | tf_op jit(solution)/shard_map/reduce_scatter | solution.py:94
  353.7 8.6 %slice-start = ((s8[8388608]{0:T(1024)(128)(4,1)}), s8[4194304]{0:T(1024)(128)(4,1)S(1)}, s32[]{:S(2)}) async-start(s8[8388608]{0:T(1024)(128)(4,1)} %bitcast.56), calls=%async_computation.5 | async-start | bytes 8388608
  353.7 8.6 %slice-start.1 = ((s8[8388608]{0:T(1024)(128)(4,1)}), s8[4194304]{0:T(1024)(128)(4,1)S(1)}, s32[]{:S(2)}) async-start(s8[8388608]{0:T(1024)(128)(4,1)} %bitcast.56), calls=%async_computation.6 | async-start | bytes 8388608
  362.3 51.6 %copy-start.1 = (bf16[64,512,16]{1,2,0:T(8,128)(2,1)S(1)}, bf16[64,512,16]{1,2,0:T(8,128)(2,1)}, u32[]{:S(2)}) copy-start(bf16[64,512,16]{1,2,0:T(8,128)(2,1)} %param.12) | copy-start | bytes 3145732
Sparse Core Ops, SparseCore 0:
  21.7 128.1 all-gather.2
  339.0 74.8 reduce-scatter.2
where the time goes:
time: 424 us; the launch traced here: 421 us
  blocking collectives  291 us (69%)
  waiting for transfers between devices  44.1 us (10%)
  matrix products  30.8 us (7%)
  local copies, waits for them, and re-layouts  21.3 us (5%)
  between operations  16.2 us (4%)
  starting transfers between devices  14.4 us (3%)
    all_gather x1, blocking collectives, local(): grad_all = lax.all_gather(grad_flat, 'dp', axis=0, tiled=True)  148 us
    unnamed x2, blocking collectives  142 us
    reduce_scatter x1, waiting for transfers between devices, local(): lax.psum_scatter(partial_up_gradient.reshape(number_of_adapters, adapter_...  43.4 us
  transfers between devices with their start and end apart: 4, of which 1 were waited for; matrix products, arithmetic and copies ran while one was open for 12% of the time, Pallas kernels for 0%

commit v1 on v0

v1 whole, which is shorter than its diff:
```python
import jax
import jax.numpy as jnp
from jax import lax
from jax.sharding import PartitionSpec as P

adapter_scale = 2.0


def local(
    tokens,
    cotangent,
    frozen_weight,
    frozen_scale,
    adapter_down_weight,
    adapter_up_weight,
    sequence_adapter,
    sequence_token_length,
):
    f32, bf16 = jnp.float32, jnp.bfloat16
    tok_count, width = tokens.shape
    seqs = sequence_adapter.shape[0]
    slot = tok_count // seqs
    adapters, shard_width, rank = adapter_down_weight.shape
    out_width = frozen_weight.shape[1]
    n = lax.axis_size("dp")
    scale = frozen_scale[0]

    every_index = lax.all_gather(sequence_adapter, "dp", axis=0, tiled=True)
    total = every_index.shape[0]
    weight = lax.all_gather(frozen_weight, "dp", axis=0, tiled=True)

    down_t = jnp.swapaxes(adapter_down_weight, 1, 2)
    chosen = down_t[every_index].reshape(total * rank, shard_width)
    own_down = lax.all_to_all(chosen, "dp", split_axis=0, concat_axis=1, tiled=True)
    own_down = own_down.reshape(seqs, rank, width)

    positions = lax.broadcasted_iota(jnp.int32, (seqs, slot), 1)
    live = (positions < sequence_token_length[:, None])[:, :, None]
    masked_cot = jnp.where(
        live, cotangent.reshape(seqs, slot, out_width), jnp.zeros((), bf16)
    )
    own_up = adapter_up_weight[sequence_adapter]
    grad_rank = (
        adapter_scale
        * jnp.einsum("spo,sro->spr", masked_cot, own_up, preferred_element_type=f32)
    ).astype(bf16)
    tokens_seq = tokens.reshape(seqs, slot, width)

    down_terms = jnp.einsum(
        "spr,spc->src", grad_rank, tokens_seq, preferred_element_type=f32
    )
    down_all = lax.all_to_all(
        down_terms.reshape(seqs * rank, width), "dp", split_axis=1, concat_axis=0, tiled=True
    )

    rank_vals = jnp.einsum(
        "spc,src->spr", tokens_seq, own_down, preferred_element_type=f32
    ).astype(bf16)
    up_terms = jnp.einsum(
        "spr,spo->sro", rank_vals, masked_cot, preferred_element_type=f32
    )
    up_all = lax.all_to_all(
        up_terms.reshape(seqs * rank, out_width), "dp", split_axis=1, concat_axis=0, tiled=True
    )

    select = (every_index[None, :] == jnp.arange(adapters, dtype=jnp.int32)[:, None]).astype(f32)
    down_grad = jnp.dot(
        select, down_all.reshape(total, rank * shard_width), precision=lax.Precision.HIGHEST
    ).reshape(adapters, rank, shard_width)
    down_grad = jnp.swapaxes(down_grad, 1, 2)
    up_grad = (
        adapter_scale
        * jnp.dot(
            select, up_all.reshape(total, rank * (out_width // n)), precision=lax.Precision.HIGHEST
        )
    ).reshape(adapters, rank, out_width // n)

    adapter_out = jnp.einsum("spr,sro->spo", rank_vals, own_up, preferred_element_type=f32)
    base_out = jnp.dot(tokens, weight, preferred_element_type=f32)
    combined = scale * base_out.reshape(seqs, slot, out_width) + adapter_scale * adapter_out
    projection = jnp.where(live, combined, 0.0).astype(bf16).reshape(tok_count, out_width)

    lora_back = jnp.einsum("spr,src->spc", grad_rank, own_down, preferred_element_type=f32).astype(bf16)
    base_back = lax.dot_general(
        masked_cot.reshape(tok_count, out_width),
        weight,
        (((1,), (1,)), ((), ())),
        preferred_element_type=f32,
    )
    token_grad = (
        scale * base_back + lora_back.reshape(tok_count, width).astype(f32)
    ).astype(bf16)
    return projection, token_grad, down_grad, up_grad


def solution(mesh):
    placed = (
        P(("groups", "dp"), None),
        P(("groups", "dp"), None),
        P("dp", None),
        P(),
        P("groups", "dp", None),
        P("groups", None, None),
        P(("groups", "dp")),
        P(("groups", "dp")),
    )
    return jax.shard_map(
        local,
        mesh=mesh,
        in_specs=placed,
        out_specs=(
            P(("groups", "dp"), None),
            P(("groups", "dp"), None),
            P("groups", "dp", None),
            P("groups", None, "dp"),
        ),
        check_vma=False,
    )
```

time: 424 us -> 141 us (0.33)
  blocking collectives: 291 us -> 8.87 us
  waiting for transfers between devices: 44.1 us -> 53.9 us
  local copies, waits for them, and re-layouts: 21.3 us -> 14.5 us
  matrix products: 30.8 us -> 26.2 us
    all_gather x1 -> x0, blocking collectives: 148 us -> none  [local(): grad_all = lax.all_gather(grad_flat, 'dp', axis=0, tiled=True)]
    unnamed x2 -> x1, blocking collectives: 142 us -> 8.87 us
    all_to_all x2 -> x3, waiting for transfers between devices: 0.01 us -> 53.2 us  [the longest x1 33.8 us: local(): lax.all_to_all(down_terms.reshape(seqs * rank, width), 'dp', split_axis=1...]
    reduce_scatter x1 -> x0, waiting for transfers between devices: 43.4 us -> none  [local(): lax.psum_scatter(partial_up_gradient.reshape(number_of_adapters, adapter_...]
    convert_element_type x4 -> x0, local copies, waits for them, and re-layouts: 5.52 us -> none  [the longest x1 4.26 us: local(): adapter_input_grad.astype(jnp.float32)]
    dot_general x10, matrix products: 30.8 us -> 26.2 us  [the longest x1 7.11 us: local(): base_out = jnp.dot(tokens, weight, preferred_element_type=f32)]
    all_to_all x2 -> x3, starting transfers between devices: 14.4 us -> 17.6 us  [the longest x1 7.83 us: local(): lax.all_to_all(chosen, 'dp', split_axis=0, concat_axis=1, tiled=True)]
  transfers between devices with their start and end apart: 4 -> 4, of which waited for: 1 -> 3; matrix products, arithmetic and copies ran while one was open for 12% -> 22% of each run, Pallas kernels for 0% -> 0%
where the time goes in v1:
time: 141 us; the launch traced here: 139 us
  waiting for transfers between devices  53.9 us (38%)
  matrix products  26.2 us (19%)
  starting transfers between devices  17.7 us (13%)
  between operations  15.5 us (11%)
  local copies, waits for them, and re-layouts  14.5 us (10%)
  blocking collectives  8.87 us (6%)
  other arithmetic  2.21 us (2%)
    all_to_all x1, waiting for transfers between devices, local(): lax.all_to_all(down_terms.reshape(seqs * rank, width), 'dp', split_axis=1...  33.8 us
    all_to_all x1, waiting for transfers between devices, local(): lax.all_to_all(chosen, 'dp', split_axis=0, concat_axis=1, tiled=True)  17.5 us
    unnamed x1, blocking collectives  8.87 us
    all_to_all x1, starting transfers between devices, local(): lax.all_to_all(chosen, 'dp', split_axis=0, concat_axis=1, tiled=True)  7.83 us
    dot_general x1, matrix products, local(): base_out = jnp.dot(tokens, weight, preferred_element_type=f32)  7.11 us
    unnamed x15, local copies, waits for them, and re-layouts  6.38 us
    all_to_all x1, starting transfers between devices, local(): lax.all_to_all(up_terms.reshape(seqs * rank, out_width), 'dp', split_axis...  5.02 us
    all_to_all x1, starting transfers between devices, local(): lax.all_to_all(down_terms.reshape(seqs * rank, width), 'dp', split_axis=1...  4.78 us
  transfers between devices with their start and end apart: 4, of which 3 were waited for; matrix products, arithmetic and copies ran while one was open for 22% of the time, Pallas kernels for 0%

profile of v1, /device:TPU:5, one launch (start us, length us, event | category | flops | bytes accessed | tf_op | source)
XLA Modules:
  0.0 138.8 jit_solution(13881186489771652481)
XLA Ops:
  7.2 0.7 all-gather.2.cloned.1.call-update
  7.9 1.2 dynamic-slice
  9.8 0.9 dynamic-update-slice
  10.7 8.9 %all-reduce = s32[32]{0:T(128)S(1)} all-reduce(s32[32]{0:T(128)S(1)} %dynamic-update-slice), channel_id=1, replica_groups=mesh['groups'=2,'dp'=16] {'dp'}, use_global_device_ids=true, to_apply=%add | all-reduce | flops 32 | bytes 256
  19.6 1.4 gather_fusion
  20.9 7.8 %all-to-all-start = ((bf16[16,32,512]{2,1,0:T(8,128)(2,1)}), bf16[16,32,512]{2,1,0:T(8,128)(2,1)S(1)}, u32[]{:S(2)}, u32[]{:S(2)}) async-start(bf16[16,32,512]{2,1,0:T(8,128)(2,1)} %bitcast.4), calls=%async_computation | async-start | bytes 1048576 | tf_op jit(solution)/shard_map/all_to_all | solution.py:34
  28.8 0.7 compare_select_fusion
  29.4 1.8 %gather_fusion.1 = bf16[2,16,512]{2,1,0:T(8,128)(2,1)S(1)} fusion(bf16[64,16,512]{2,1,0:T(8,128)(2,1)} %param.13, s32[1024]{0:T(1024)S(1)} %pad_clamp_fusion), kind=kCustom, calls=%fused_computation.1 | custom fusion | bytes 65544 | tf_op jit(solution)/shard_map/gather | solution.py:42
  31.2 0.7 fusion.21
  32.0 1.2 fusion.5
  33.2 17.5 %all-to-all-done = bf16[16,32,512]{2,1,0:T(8,128)(2,1)S(1)} async-done(((bf16[16,32,512]{2,1,0:T(8,128)(2,1)}), bf16[16,32,512]{2,1,0:T(8,128)(2,1)S(1)}, u32[]{:S(2)}, u32[]{:S(2)}) %all-to-all-start) | async-done | bytes 524320 | tf_op jit(solution)/shard_map/all_to_all | solution.py:34
  50.6 0.3 copy.21
  51.2 3.4 %convolution_convert_fusion.1 = bf16[2,16,128]{2,1,0:T(8,128)(2,1)S(1)} fusion(bf16[2,16,8192]{2,1,0:T(8,128)(2,1)S(1)} %reshape.81, bf16[2,128,8192]{2,1,0:T(8,128)(2,1)} %bitcast.52), kind=kOutput, calls=%fused_computation.15 | convolution fusion | flops 67112960 | bytes 4726784 | tf_op jit(solution)/shard_map/spc,src->spr/dot_general | solution.py:56
  55.0 0.8 reshape.113
  55.8 5.0 %all-to-all-start.2 = ((f32[16,1,1024]{2,1,0:T(1,128)}), f32[16,1,1024]{2,1,0:T(1,128)S(1)}, u32[]{:S(2)}, u32[]{:S(2)}) async-start(f32[16,1,1024]{2,1,0:T(1,128)} %reshape.113), calls=%async_computation.2 | async-start | bytes 131072 | tf_op jit(solution)/shard_map/all_to_all | solution.py:62
  60.8 2.9 %fusion.22 = f32[2,16,8192]{2,1,0:T(8,128)S(1)} fusion(bf16[2,128,16]{1,2,0:T(8,128)(2,1)S(1)} %fusion.5, bf16[2,128,8192]{2,1,0:T(8,128)(2,1)} %bitcast.53), kind=kOutput, calls=%fused_computation.40 | convolution fusion | flops 67108864 | bytes 5251072 | tf_op jit(solution)/shard_map/spr,spc->src/dot_general | solution.py:49
  63.7 0.6 copy.28
  64.3 1.6 %copy.22 = f32[32,16,512]{2,0,1:T(8,128)} copy(f32[32,16,512]{2,1,0:T(8,128)S(1)} %bitcast.58) | data formatting | bytes 2097152 | tf_op jit(solution)/shard_map/all_to_all | solution.py:52
  65.9 1.9 %all-to-all-done.2 = f32[16,1,1024]{2,1,0:T(1,128)S(1)} async-done(((f32[16,1,1024]{2,1,0:T(1,128)}), f32[16,1,1024]{2,1,0:T(1,128)S(1)}, u32[]{:S(2)}, u32[]{:S(2)}) %all-to-all-start.2) | async-done | bytes 65568 | tf_op jit(solution)/shard_map/all_to_all | solution.py:62
  67.9 4.8 %all-to-all-start.1 = ((f32[32,16,512]{2,0,1:T(8,128)}), f32[32,16,512]{2,0,1:T(8,128)S(1)}, u32[]{:S(2)}, u32[]{:S(2)}) async-start(f32[32,16,512]{2,0,1:T(8,128)} %copy.22), calls=%async_computation.1 | async-start | bytes 2097152 | tf_op jit(solution)/shard_map/all_to_all | solution.py:52
  73.3 3.3 %convolution_convert_fusion = bf16[2,128,8192]{2,1,0:T(8,128)(2,1)} fusion(bf16[2,128,16]{1,2,0:T(8,128)(2,1)S(1)} %fusion.5, bf16[2,16,8192]{2,1,0:T(8,128)(2,1)S(1)} %reshape.81), kind=kOutput, calls=%fused_computation.5 | convolution fusion | flops 69206016 | bytes 4726784 | tf_op jit(solution)/shard_map/spr,src->spc/dot_general | solution.py:83
  76.6 0.5 broadcast.39
  77.1 0.8 reduce
  78.2 0.3 convolution_multiply_fusion.3
  78.5 0.8 copy.25
  79.4 33.8 %all-to-all-done.1 = f32[32,16,512]{2,0,1:T(8,128)S(1)} async-done(((f32[32,16,512]{2,0,1:T(8,128)}), f32[32,16,512]{2,0,1:T(8,128)S(1)}, u32[]{:S(2)}, u32[]{:S(2)}) %all-to-all-start.1) | async-done | bytes 1048608 | tf_op jit(solution)/shard_map/all_to_all | solution.py:52
  113.2 1.2 reshape.85
  114.3 2.3 %convolution_bitcast_fusion = f32[64,512,16]{1,0,2:T(8,128)S(1)} fusion(f32[4,16,8,512]{3,2,1,0:T(8,128)} %bitcast.57, s32[32]{0:T(128)S(1)} %all-reduce), kind=kOutput, calls=%fused_computation.6 | convolution fusion | flops 201328640 | bytes 3145856 | tf_op jit(solution)/shard_map/dot_general | solution.py:67
  116.7 2.5 %copy.26 = f32[64,512,16]{1,2,0:T(8,128)} copy(f32[64,512,16]{1,0,2:T(8,128)S(1)} %convolution_bitcast_fusion) | data formatting | bytes 4194304
  119.2 7.1 %convolution_multiply_fusion.2 = f32[256,512]{1,0:T(8,128)S(1)} fusion(bf16[256,8192]{1,0:T(8,128)(2,1)} %param.8, bf16[8192,512]{1,0:T(8,128)(2,1)} %all-gather.2.cloned.1.call-done, f32[]{:T(128)} %bitcast.49), kind=kOutput, calls=%fused_computation.10 | convolution fusion | flops 2147614720 | bytes 13107204 | tf_op jit(solution)/shard_map/dot_general | solution.py:79
  126.3 1.0 fusion.4
  127.5 4.4 %fusion.1 = bf16[256,8192]{1,0:T(8,128)(2,1)} fusion(bf16[8192,512]{1,0:T(8,128)(2,1)S(1)} %copy-done.2, bf16[256,8192]{1,0:T(8,128)(2,1)S(1)} %bitcast.55, f32[]{:T(128)} %bitcast.50, bf16[256,512]{1,0:T(8,128)(2,1)S(1)} %copy-done.3, pred[256]{0:T(512)(128)(4,1)S(1)} %get-tuple-element.16), kind=kOutput, calls=%fused_computation.4 | convolution fusion | flops 2156003328 | bytes 17039620 | tf_op jit(solution)/shard_map/dot_general | solution.py:84
  (21 shorter events, 1.2 us)
Async XLA Ops:
  7.2 12.4 %copy-start = (bf16[64,512,16]{1,2,0:T(8,128)(2,1)S(1)}, bf16[64,512,16]{1,2,0:T(8,128)(2,1)}, u32[]{:S(2)}) copy-start(bf16[64,512,16]{1,2,0:T(8,128)(2,1)} %param.12) | copy-start | bytes 3145732
  7.2 112.0 %all-gather.2.cloned.1.call-start = ((), (), s32[]{:S(2)}) async-start(), calls=%async_computation.3 | async-start | bytes 8912896 | tf_op jit(solution)/shard_map/all_gather | solution.py:30
  20.9 33.6 %copy-start.3 = (bf16[256,512]{1,0:T(8,128)(2,1)S(1)}, bf16[256,512]{1,0:T(8,128)(2,1)}, u32[]{:S(2)}) copy-start(bf16[256,512]{1,0:T(8,128)(2,1)} %param.9) | copy-start | bytes 786436
  20.9 29.7 %all-to-all-start = ((bf16[16,32,512]{2,1,0:T(8,128)(2,1)}), bf16[16,32,512]{2,1,0:T(8,128)(2,1)S(1)}, u32[]{:S(2)}, u32[]{:S(2)}) async-start(bf16[16,32,512]{2,1,0:T(8,128)(2,1)} %bitcast.4), calls=%async_computation | async-start | bytes 1048576 | tf_op jit(solution)/shard_map/all_to_all | solution.py:34
  55.8 12.1 %all-to-all-start.2 = ((f32[16,1,1024]{2,1,0:T(1,128)}), f32[16,1,1024]{2,1,0:T(1,128)S(1)}, u32[]{:S(2)}, u32[]{:S(2)}) async-start(f32[16,1,1024]{2,1,0:T(1,128)} %reshape.113), calls=%async_computation.2 | async-start | bytes 131072 | tf_op jit(solution)/shard_map/all_to_all | solution.py:62
  67.9 45.3 %all-to-all-start.1 = ((f32[32,16,512]{2,0,1:T(8,128)}), f32[32,16,512]{2,0,1:T(8,128)S(1)}, u32[]{:S(2)}, u32[]{:S(2)}) async-start(f32[32,16,512]{2,0,1:T(8,128)} %copy.22), calls=%async_computation.1 | async-start | bytes 2097152 | tf_op jit(solution)/shard_map/all_to_all | solution.py:52
  119.2 8.1 %copy-start.1 = (bf16[2,128,8192]{2,1,0:T(8,128)(2,1)S(1)}, bf16[2,128,8192]{2,1,0:T(8,128)(2,1)}, u32[]{:S(2)}) copy-start(bf16[2,128,8192]{2,1,0:T(8,128)(2,1)} %convolution_convert_fusion) | copy-start | bytes 12582916
  119.2 8.3 %copy-start.2 = (bf16[8192,512]{1,0:T(8,128)(2,1)S(1)}, bf16[8192,512]{1,0:T(8,128)(2,1)}, u32[]{:S(2)}) copy-start(bf16[8192,512]{1,0:T(8,128)(2,1)} %all-gather.2.cloned.1.call-done) | copy-start | bytes 25165828
Sparse Core Ops, SparseCore 0:
  10.2 105.0 all-gather.1

commit v2 on v1

--- a/solution.py
+++ b/solution.py
@@ -1,10 +1,392 @@
+import functools
+
 import jax
 import jax.numpy as jnp
 from jax import lax
+from jax.experimental import pallas as pl
+from jax.experimental.pallas import tpu as pltpu
 from jax.sharding import PartitionSpec as P
 
 adapter_scale = 2.0
-
+NT = (((1,), (1,)), ((), ()))
+TN = (((0,), (0,)), ((), ()))
+
+
+def exchange(
+    n, slot, rank,
+    lens_ref, own_idx_ref, scale_ref, tok_ref, cot_ref, w_ref, down_ref, up_ref,
+    proj_ref, tig_ref, idx_all, drecv, urecv,
+    wbuf, od, csend, dsend, usend, idx_send, idx_sm, mc_ref, g_ref, acc, rk,
+    local_sem, idx_s, idx_r, c_s, c_r, d_s, d_r, u_s, u_r, ring_s, ring_r, twin_s, twin_r,
+):
+    f32, bf16 = jnp.float32, jnp.bfloat16
+    me = lax.axis_index("dp")
+    rows, width = tok_ref.shape
+    seqs = rows // slot
+    depth = w_ref.shape[0]
+    quarter, half = depth // 4, depth // 2
+    chips = n // 2
+    side = chips // 2
+    core = lax.rem(me, 2)
+    twin = me + 1 - 2 * core
+    chip = me // 2
+    pz, py = chip // 2, lax.rem(chip, 2)
+    pos = pz + py * (2 * side - 1 - 2 * pz)
+
+    def chip_at(p):
+        p = lax.rem(p + 2 * chips, chips)
+        y = p // side
+        z = p + y * (2 * side - 1 - 2 * p)
+        return 2 * z + y
+
+    ahead = chip_at(pos + 1) * 2 + core
+    behind = chip_at(pos - 1) * 2 + core
+
+    def remote(src, dst, s, r, dev):
+        return pltpu.make_async_remote_copy(
+            src_ref=src, dst_ref=dst, send_sem=s, recv_sem=r,
+            device_id={"dp": dev}, device_id_type=pl.DeviceIdType.MESH,
+        )
+
+    barrier = pltpu.get_barrier_semaphore()
+
+    @pl.loop(1, n)
+    def _(j):
+        pl.semaphore_signal(
+            barrier, inc=1, device_id={"dp": lax.rem(me + j, n)},
+            device_id_type=pl.DeviceIdType.MESH,
+        )
+
+    lane = lax.broadcasted_iota(jnp.int32, (8, 128), 1)
+    tile = jnp.zeros((8, 128), jnp.int32)
+    for s in range(seqs):
+        tile = jnp.where(lane == s, own_idx_ref[s], tile)
+    idx_send[...] = tile
+    pl.semaphore_wait(barrier, n - 1)
+
+    def shard_of(q, t):
+        return chip_at(pos - t if q < 2 else pos + t) * 2 + core
+
+    def rows_of(shard, q):
+        return pl.ds(pl.multiple_of(shard * depth + q * quarter, quarter), quarter)
+
+    def ring_copy(q, t):
+        at = rows_of(shard_of(q, t), q)
+        return remote(wbuf.at[at], wbuf.at[at], ring_s.at[q, t], ring_r.at[q, t],
+                      ahead if q < 2 else behind)
+
+    def twin_copy(q, t):
+        at = rows_of(shard_of(q, t), q)
+        return remote(wbuf.at[at], wbuf.at[at], twin_s.at[q, t], twin_r.at[q, t], twin)
+
+    def ring_wait(q, t):
+        at = rows_of(shard_of(q, t), q)
+        remote(wbuf.at[at], wbuf.at[at], ring_s.at[q, t - 1], ring_r.at[q, t - 1],
+               ahead if q < 2 else behind).wait_recv()
+
+    def twin_wait(q, t):
+        at = rows_of(shard_of(q, t) + 1 - 2 * core, q)
+        at = rows_of(shard_of(q, t) + 1 - 2 * core, q)
+        remote(wbuf.at[at], wbuf.at[at], twin_s.at[q, t], twin_r.at[q, t], twin).wait_recv()
+
+    own_rows = pl.ds(pl.multiple_of(me * depth, depth), depth)
+    own = pltpu.make_async_copy(w_ref, wbuf.at[own_rows], local_sem.at[0])
+    own.start()
+    own.wait()
+    for q in (0, 2, 1, 3):
+        ring_copy(q, 0).start()
+    for q in range(4):
+        twin_copy(q, 0).start()
+
+    def idx_copy(j, block):
+        return remote(idx_send, idx_all.at[block], idx_s.at[j], idx_r.at[j], lax.rem(me + j, n))
+
+    @pl.loop(1, n)
+    def _(j):
+        idx_copy(j, me).start()
+
+    idx_own = pltpu.make_async_copy(idx_send, idx_all.at[me], local_sem.at[1])
+    idx_own.start()
+
+    row = lax.broadcasted_iota(jnp.int32, (rows, 1), 0)
+    live = row < lens_ref[0]
+    for s in range(1, seqs):
+        live = live | ((row >= s * slot) & (row < s * slot + lens_ref[s]))
+    mc = jnp.where(live, cot_ref[...].astype(f32), 0.0).astype(bf16)
+    mc_ref[...] = mc
+    r2 = lax.broadcasted_iota(jnp.int32, (rows, seqs * rank), 0)
+    c2 = lax.broadcasted_iota(jnp.int32, (rows, seqs * rank), 1)
+    diag = (r2 < slot) & (c2 < rank)
+    for s in range(1, seqs):
+        diag = diag | ((r2 >= s * slot) & (r2 < (s + 1) * slot)
+                       & (c2 >= s * rank) & (c2 < (s + 1) * rank))
+    up2 = jnp.concatenate([up_ref[own_idx_ref[s]] for s in range(seqs)], axis=0)
+    g = adapter_scale * lax.dot_general(mc, up2, NT, preferred_element_type=f32)
+    g_ref[...] = jnp.where(diag, g, 0.0).astype(bf16)
+
+    idx_own.wait()
+
+    @pl.loop(1, n)
+    def _(j):
+        idx_copy(j, lax.rem(me - j + n, n)).wait_recv()
+
+    to_smem = pltpu.make_async_copy(idx_all, idx_sm, local_sem.at[1])
+    to_smem.start()
+    to_smem.wait()
+
+    def c_copy(j, block):
+        dev = lax.rem(me + j, n)
+        return remote(csend.at[dev], od.at[block], c_s.at[j], c_r.at[j], dev)
+
+    for s in range(seqs):
+        od[me, pl.ds(s * rank, rank), :] = down_ref[own_idx_ref[s]]
+
+    @pl.loop(1, n)
+    def _(j):
+        dev = lax.rem(me + j, n)
+        for s in range(seqs):
+            csend[dev, pl.ds(s * rank, rank), :] = down_ref[idx_sm[dev, 0, s]]
+        c_copy(j, me).start()
+
+    def forward(t, last):
+        for q in (0, 2, 1, 3):
+            ring_wait(q, t)
+            if not last:
+                ring_copy(q, t).start()
+            twin_copy(q, t).start()
+
+    def column(shard, h):
+        return pl.ds(pl.multiple_of(shard * depth + h * half, half), half)
+
+    def fwd(shard, h):
+        at = column(shard, h)
+        acc[...] += jnp.dot(tok_ref[:, at], wbuf[at, :], preferred_element_type=f32)
+
+    def bwd(shard, h):
+        at = column(shard, h)
+        back = lax.dot_general(mc_ref[...], wbuf[at, :], NT, preferred_element_type=f32)
+        lora = jnp.dot(g_ref[...], od[shard, :, pl.ds(h * half, half)], preferred_element_type=f32)
+        tig_ref[:, at] = (scale_ref[0] * back + lora.astype(bf16).astype(f32)).astype(bf16)
+
+    def own_part(t, fn):
+        for h in range(2):
+            fn(shard_of(2 * h, t), h)
+
+    def twin_part(t, fn):
+        for h in range(2):
+            fn(shard_of(2 * h, t) + 1 - 2 * core, h)
+
+    def twin_arrive(t):
+        for q in range(4):
+            twin_wait(q, t)
+
+    def d_copy(j, block):
+        dev = lax.rem(me + j, n)
+        return remote(dsend.at[dev], drecv.at[block], d_s.at[j], d_r.at[j], dev)
+
+    def d_term(dev):
+        at = pl.ds(pl.multiple_of(dev * depth, depth), depth)
+        dsend[dev] = lax.dot_general(g_ref[...], tok_ref[:, at], TN, preferred_element_type=f32)
+
+    def d_range(first, last):
+        @pl.loop(first, last)
+        def _(j):
+            d_term(lax.rem(me + j, n))
+            d_copy(j, me).start()
+
+    acc[...] = jnp.zeros_like(acc)
+    forward(1, False)
+    d_range(1, n // 2)
+    d_term(me)
+    d_own = pltpu.make_async_copy(dsend.at[me], drecv.at[me], local_sem.at[2])
+    d_own.start()
+    forward(2, False)
+    d_range(n // 2, n)
+    own_part(0, fwd)
+    own_part(1, fwd)
+    twin_arrive(0)
+    twin_part(0, fwd)
+    own_part(2, fwd)
+    twin_arrive(1)
+    twin_part(1, fwd)
+    forward(3, False)
+    own_part(3, fwd)
+    twin_arrive(2)
+    twin_part(2, fwd)
+
+    @pl.loop(1, n)
+    def _(j):
+        c_copy(j, lax.rem(me - j + n, n)).wait_recv()
+
+    rk[...] = jnp.zeros_like(rk)
+
+    @pl.loop(0, n)
+    def _(b):
+        at = pl.ds(pl.multiple_of(b * depth, depth), depth)
+        rk[...] += lax.dot_general(tok_ref[:, at], od[b], NT, preferred_element_type=f32)
+
+    rv = jnp.where(diag, rk[...], 0.0).astype(bf16)
+    up_t = lax.dot_general(mc_ref[...], rv, TN, preferred_element_type=f32)
+    cols = usend.shape[1]
+    for b in range(n):
+        usend[b] = up_t[b * cols:(b + 1) * cols, :]
+
+    def u_copy(j, block):
+        dev = lax.rem(me + j, n)
+        return remote(usend.at[dev], urecv.at[block], u_s.at[j], u_r.at[j], dev)
+
+    @pl.loop(1, n)
+    def _(j):
+        u_copy(j, me).start()
+
+    u_own = pltpu.make_async_copy(usend.at[me], urecv.at[me], local_sem.at[3])
+    u_own.start()
+    adapter_out = jnp.dot(rv, up2, preferred_element_type=f32)
+
+    def both(shard, h):
+        fwd(shard, h)
+        bwd(shard, h)
+
+    forward(4, False)
+
+    @pl.loop(0, 4)
+    def _(t):
+        own_part(t, bwd)
+
+    @pl.loop(0, 3)
+    def _(t):
+        twin_part(t, bwd)
+
+    @pl.loop(4, chips - 1)
+    def _(t):
+        twin_arrive(t - 1)
+        own_part(t, both)
+        twin_part(t - 1, both)
+
+        @pl.when(t < chips - 2)
+        def _():
+            forward(t + 1, False)
+
+    forward(chips - 1, True)
+    own_part(chips - 1, both)
+    twin_arrive(chips - 2)
+    twin_part(chips - 2, both)
+    twin_arrive(chips - 1)
+    twin_part(chips - 1, both)
+    out = scale_ref[0] * acc[...] + adapter_scale * adapter_out
+    proj_ref[...] = jnp.where(live, out, 0.0).astype(bf16)
+
+    d_own.wait()
+    u_own.wait()
+
+    @pl.loop(1, n)
+    def _(j):
+        back = lax.rem(me - j + n, n)
+        d_copy(j, back).wait_recv()
+        u_copy(j, back).wait_recv()
+        idx_copy(j, me).wait_send()
+        c_copy(j, me).wait_send()
+        d_copy(j, me).wait_send()
+        u_copy(j, me).wait_send()
+
+    @pl.loop(0, chips)
+    def _(t):
+        for q in range(4):
+            twin_copy(q, t).wait_send()
+
+    @pl.loop(0, chips - 1)
+    def _(t):
+        for q in range(4):
+            ring_copy(q, t).wait_send()
+
+
+def gather_adapters(idx_ref, d_ref, out_ref):
+    out_ref[...] = jnp.zeros_like(out_ref)
+
+    @pl.loop(0, d_ref.shape[0])
+    def _(k):
+        i = idx_ref[k]
+        out_ref[i] = out_ref[i] + d_ref[k]
+
+
+def local_ring(
+    n,
+    tokens,
+    cotangent,
+    frozen_weight,
+    frozen_scale,
+    adapter_down_weight,
+    adapter_up_weight,
+    sequence_adapter,
+    sequence_token_length,
+):
+    f32, bf16 = jnp.float32, jnp.bfloat16
+    rows, width = tokens.shape
+    seqs = sequence_adapter.shape[0]
+    slot = rows // seqs
+    adapters, depth, rank = adapter_down_weight.shape
+    out_width = frozen_weight.shape[1]
+    cols = out_width // n
+    chips = n // 2
+    sr = seqs * rank
+    total = n * seqs
+    vmem = pl.BlockSpec(memory_space=pltpu.VMEM)
+    smem = pl.BlockSpec(memory_space=pltpu.SMEM)
+    hbm = pl.BlockSpec(memory_space=pl.ANY)
+    dma = pltpu.SemaphoreType.DMA
+    proj, tig, idx_all, drecv, urecv = pl.pallas_call(
+        functools.partial(exchange, n, slot, rank),
+        out_shape=(
+            jax.ShapeDtypeStruct((rows, out_width), bf16),
+            jax.ShapeDtypeStruct((rows, width), bf16),
+            jax.ShapeDtypeStruct((n, 8, 128), jnp.int32),
+            jax.ShapeDtypeStruct((n, sr, depth), f32),
+            jax.ShapeDtypeStruct((n, cols, sr), f32),
+        ),
+        in_specs=[smem, smem, smem, vmem, vmem, vmem, vmem, vmem],
+        out_specs=(vmem, vmem, hbm, hbm, hbm),
+        scratch_shapes=[
+            pltpu.VMEM((width, out_width), bf16),
+            pltpu.VMEM((n, sr, depth), bf16),
+            pltpu.VMEM((n, sr, depth), bf16),
+            pltpu.VMEM((n, sr, depth), f32),
+            pltpu.VMEM((n, cols, sr), f32),
+            pltpu.VMEM((8, 128), jnp.int32),
+            pltpu.SMEM((n, 8, 128), jnp.int32),
+            pltpu.VMEM((rows, out_width), bf16),
+            pltpu.VMEM((rows, sr), bf16),
+            pltpu.VMEM((rows, out_width), f32),
+            pltpu.VMEM((rows, sr), f32),
+            dma((4,)),
+            dma((n,)), dma((n,)), dma((n,)), dma((n,)),
+            dma((n,)), dma((n,)), dma((n,)), dma((n,)),
+            dma((4, chips)), dma((4, chips)), dma((4, chips)), dma((4, chips)),
+        ],
+        compiler_params=pltpu.CompilerParams(
+            collective_id=0, has_side_effects=True, vmem_limit_bytes=48 * 2**20
+        ),
+        cost_estimate=pl.CostEstimate(
+            flops=4 * rows * width * out_width, bytes_accessed=2 * rows * width * 2,
+            transcendentals=0,
+        ),
+    )(
+        sequence_token_length, sequence_adapter, frozen_scale, tokens, cotangent,
+        frozen_weight, jnp.swapaxes(adapter_down_weight, 1, 2), adapter_up_weight,
+    )
+    every_index = idx_all[:, 0, :seqs].reshape(total)
+    down_grad = pl.pallas_call(
+        gather_adapters,
+        out_shape=jax.ShapeDtypeStruct((adapters, rank, depth), f32),
+        in_specs=[smem, vmem],
+        out_specs=vmem,
+        compiler_params=pltpu.CompilerParams(vmem_limit_bytes=16 * 2**20),
+    )(every_index, drecv.reshape(total, rank, depth))
+    select = (every_index[None, :] == jnp.arange(adapters, dtype=jnp.int32)[:, None]).astype(f32)
+    up_seq = jnp.transpose(urecv.reshape(n, cols, seqs, rank), (0, 2, 3, 1)).reshape(total, rank * cols)
+    up_grad = (
+        adapter_scale * jnp.dot(select, up_seq, precision=lax.Precision.HIGHEST)
+    ).reshape(adapters, rank, cols)
+    return proj, tig, jnp.swapaxes(down_grad, 1, 2), up_grad
 
 def local(
     tokens,
@@ -104,8 +486,10 @@
         P(("groups", "dp")),
         P(("groups", "dp")),
     )
+    n = mesh.shape["dp"]
+    ring = n % 4 == 0 and n >= 12 and n <= 32
     return jax.shard_map(
-        local,
+        functools.partial(local_ring, n) if ring else local,
         mesh=mesh,
         in_specs=placed,
         out_specs=(

time: 141 us -> 116 us (0.82)
  Pallas kernels: 0 us -> 101 us
  waiting for transfers between devices: 53.9 us -> 0 us
  matrix products: 26.2 us -> 0.2 us
  starting transfers between devices: 17.7 us -> 0 us
  between operations: 15.5 us -> 1.33 us
  blocking collectives: 8.87 us -> 0 us
  other arithmetic: 2.21 us -> 0 us
  local copies, waits for them, and re-layouts: 14.5 us -> 12.3 us
    pallas_call x0 -> x2, Pallas kernels: none -> 101 us  [the longest x1 98.3 us: local_ring(): pl.pallas_call(functools.partial(exchange, n, slot, rank), out_shape=(jax...]
    all_to_all x3 -> x0, waiting for transfers between devices: 53.2 us -> none  [the longest x1 33.8 us: local(): lax.all_to_all(down_terms.reshape(seqs * rank, width), 'dp', split_axis=1...]
    dot_general x10 -> x1, matrix products: 26.2 us -> 0.2 us  [local_ring(): jnp.dot(select, up_seq, precision=lax.Precision.HIGHEST)]
    all_to_all x3 -> x0, starting transfers between devices: 17.6 us -> none  [the longest x1 7.83 us: local(): lax.all_to_all(chosen, 'dp', split_axis=0, concat_axis=1, tiled=True)]
    unnamed x1 -> x0, blocking collectives: 8.87 us -> none
    unnamed x15 -> x14, local copies, waits for them, and re-layouts: 6.38 us -> 11.1 us
    gather x2 -> x0, local copies, waits for them, and re-layouts: 3.15 us -> none  [the longest x1 1.77 us: local(): own_up = adapter_up_weight[sequence_adapter]]
    all_to_all x6 -> x0, local copies, waits for them, and re-layouts: 2.61 us -> none  [the longest x1 1.58 us: local(): lax.all_to_all(down_terms.reshape(seqs * rank, width), 'dp', split_axis=1...]
  transfers between devices with their start and end apart: 4 -> 0, of which waited for: 3 -> 0; matrix products, arithmetic and copies ran while one was open for 22% -> 0% of each run, Pallas kernels for 0% -> 0%
where the time goes in v2:
time: 116 us; the launch traced here: 114 us
  Pallas kernels  101 us (87%)
  local copies, waits for them, and re-layouts  12.3 us (11%)
  between operations  1.33 us (1%)
    pallas_call x1, Pallas kernels, local_ring(): pl.pallas_call(functools.partial(exchange, n, slot, rank), out_shape=(jax...  98.3 us
    unnamed x14, local copies, waits for them, and re-layouts  11.1 us

profile of v2, /device:TPU:5, one launch (start us, length us, event | category | flops | bytes accessed | tf_op | source)
XLA Modules:
  0.0 114.4 jit_solution(6991594523884133165)
XLA Ops:
  1.3 0.0 copy-start
  1.3 1.2 %copy-done = bf16[64,512,16]{1,2,0:T(8,128)(2,1)S(1)} copy-done((bf16[64,512,16]{1,2,0:T(8,128)(2,1)S(1)}, bf16[64,512,16]{1,2,0:T(8,128)(2,1)}, u32[]{:S(2)}) %copy-start) | copy-done | bytes 1048600
  2.5 0.0 copy-start.1
  2.5 1.2 %copy-done.1 = bf16[64,16,512]{2,1,0:T(8,128)(2,1)S(1)} copy-done((bf16[64,16,512]{2,1,0:T(8,128)(2,1)S(1)}, bf16[64,16,512]{2,1,0:T(8,128)(2,1)}, u32[]{:S(2)}) %copy-start.1) | copy-done | bytes 1048600
  3.7 0.0 copy-start.2
  3.7 1.0 copy-done.2
  4.8 0.0 copy-start.3
  4.8 0.9 copy-done.3
  5.7 0.0 copy-start.4
  5.7 0.7 copy-done.4
  6.4 0.0 copy-start.5
  6.4 0.7 copy-done.5
  7.0 98.3 %shard_map.111 = (bf16[256,512]{1,0:T(8,128)(2,1)S(1)}, bf16[256,8192]{1,0:T(8,128)(2,1)}, s32[16,8,128]{2,1,0:T(8,128)S(1)}, f32[16,32,512]{2,1,0:T(8,128)S(1)}, f32[16,32,32]{2,1,0:T(8,128)S(1)}) custom-call(s32[2]{0:T(128)S(1)} %copy-done.4, s32[2]{0:T(128)S(1)} %copy-done.5, f32[1]{0:T(128)S(6)} %copy.17.scale_ref, bf16[256,8192]{1,0:T(8,128)(2,1)} %tok_ref.1, ...), custom_call_target="tpu_custom_call" | custom-call | flops 4294967296 | bytes 8388608 | tf_op jit(solution)/shard_map/pallas_call | solution.py:337
  105.4 0.1 reshape_squeeze.3.idx_ref
  105.4 2.3 %shard_map.112 = f32[64,16,512]{2,1,0:T(8,128)} custom-call(s32[32]{0:T(128)S(1)} %reshape_squeeze.3.idx_ref, f32[32,16,512]{2,1,0:T(8,128)S(1)} %bitcast.10), custom_call_target="tpu_custom_call" | custom-call | tf_op jit(solution)/shard_map/pallas_call | solution.py:377
  107.7 0.1 copy.13
  107.8 0.1 reshape.23
  108.0 0.2 convolution_multiply_fusion
  108.2 0.8 copy.14
  109.0 0.7 copy.18
  109.7 4.6 %copy.19 = bf16[256,8192]{1,0:T(8,128)(2,1)} copy(bf16[256,8192]{1,0:T(8,128)(2,1)} %get-tuple-element.23) | data formatting | bytes 8388608
  (1 shorter events, 0.0 us)
Async XLA Ops:
  1.3 1.2 %copy-start = (bf16[64,512,16]{1,2,0:T(8,128)(2,1)S(1)}, bf16[64,512,16]{1,2,0:T(8,128)(2,1)}, u32[]{:S(2)}) copy-start(bf16[64,512,16]{1,2,0:T(8,128)(2,1)} %param.12) | copy-start | bytes 3145732
  2.5 1.2 %copy-start.1 = (bf16[64,16,512]{2,1,0:T(8,128)(2,1)S(1)}, bf16[64,16,512]{2,1,0:T(8,128)(2,1)}, u32[]{:S(2)}) copy-start(bf16[64,16,512]{2,1,0:T(8,128)(2,1)} %up_ref.1) | copy-start | bytes 3145732
  3.7 1.0 copy-start.2
  4.8 0.9 copy-start.3
  5.7 0.7 copy-start.4
  6.4 0.7 copy-start.5

commit v3 on v2

--- a/solution.py
+++ b/solution.py
@@ -14,17 +14,19 @@
 
 def exchange(
     n, slot, rank,
-    lens_ref, own_idx_ref, scale_ref, tok_ref, cot_ref, w_ref, down_ref, up_ref,
-    proj_ref, tig_ref, idx_all, drecv, urecv,
-    wbuf, od, csend, dsend, usend, idx_send, idx_sm, mc_ref, g_ref, acc, rk,
-    local_sem, idx_s, idx_r, c_s, c_r, d_s, d_r, u_s, u_r, ring_s, ring_r, twin_s, twin_r,
+    lens_ref, own_idx_ref, scale_ref, tok_hbm, cot_hbm, w_ref, down_hbm, up_hbm,
+    proj_ref, tig_hbm, idx_all, drecv, urecv,
+    tok_ref, cot_ref, down_ref, up_ref, tig_ref, wbuf, od, csend, dsend, usend, idx_send, idx_sm, mc_ref, g_ref, acc, rk,
+    local_sem, idx_s, idx_r, c_s, c_r, d_s, d_r, u_s, u_r, ring_s, ring_r, twin_s, twin_r, x_s, x_r, xt_s, xt_r, load_sem, store_sem,
 ):
     f32, bf16 = jnp.float32, jnp.bfloat16
     me = lax.axis_index("dp")
     rows, width = tok_ref.shape
     seqs = rows // slot
     depth = w_ref.shape[0]
-    quarter, half = depth // 4, depth // 2
+    half = depth // 2
+    shared, single = half * 3 // 8, half * 5 // 16
+    plane = lax.axis_index("groups")
     chips = n // 2
     side = chips // 2
     core = lax.rem(me, 2)
@@ -48,7 +50,21 @@
             device_id={"dp": dev}, device_id_type=pl.DeviceIdType.MESH,
         )
 
+    own_rows = pl.ds(pl.multiple_of(me * depth, depth), depth)
+    loads = [
+        pltpu.make_async_copy(a, b, load_sem.at[i])
+        for i, (a, b) in enumerate((
+            (w_ref, wbuf.at[own_rows]), (cot_hbm, cot_ref), (up_hbm, up_ref),
+            (down_hbm, down_ref), (tok_hbm, tok_ref),
+        ))
+    ]
+    for load in loads:
+        load.start()
+
     barrier = pltpu.get_barrier_semaphore()
+    pl.semaphore_signal(
+        barrier, inc=1, device_id={"groups": 1 - plane}, device_id_type=pl.DeviceIdType.MESH
+    )
 
     @pl.loop(1, n)
     def _(j):
@@ -62,13 +78,20 @@
     for s in range(seqs):
         tile = jnp.where(lane == s, own_idx_ref[s], tile)
     idx_send[...] = tile
-    pl.semaphore_wait(barrier, n - 1)
+    pl.semaphore_wait(barrier, n)
 
     def shard_of(q, t):
         return chip_at(pos - t if q < 2 else pos + t) * 2 + core
 
     def rows_of(shard, q):
-        return pl.ds(pl.multiple_of(shard * depth + q * quarter, quarter), quarter)
+        if q % 2 == 0:
+            return pl.ds(pl.multiple_of(shard * depth + q // 2 * half, 16), shared)
+        at = shard * depth + q // 2 * half + shared + plane * single
+        return pl.ds(pl.multiple_of(at, 16), single)
+
+    def other_rows(shard, d):
+        at = shard * depth + d * half + shared + (1 - plane) * single
+        return pl.ds(pl.multiple_of(at, 16), single)
 
     def ring_copy(q, t):
         at = rows_of(shard_of(q, t), q)
@@ -79,6 +102,20 @@
         at = rows_of(shard_of(q, t), q)
         return remote(wbuf.at[at], wbuf.at[at], twin_s.at[q, t], twin_r.at[q, t], twin)
 
+    def x_copy(d, t, at):
+        return pltpu.make_async_remote_copy(
+            src_ref=wbuf.at[at], dst_ref=wbuf.at[at], send_sem=x_s.at[d, t],
+            recv_sem=x_r.at[d, t], device_id={"groups": 1 - plane},
+            device_id_type=pl.DeviceIdType.MESH,
+        )
+
+    def x_send(d, t):
+        return x_copy(d, t, rows_of(shard_of(2 * d, t), 2 * d + 1))
+
+    def xt_copy(d, t):
+        at = other_rows(shard_of(2 * d, t), d)
+        return remote(wbuf.at[at], wbuf.at[at], xt_s.at[d, t], xt_r.at[d, t], twin)
+
     def ring_wait(q, t):
         at = rows_of(shard_of(q, t), q)
         remote(wbuf.at[at], wbuf.at[at], ring_s.at[q, t - 1], ring_r.at[q, t - 1],
@@ -86,28 +123,37 @@
 
     def twin_wait(q, t):
         at = rows_of(shard_of(q, t) + 1 - 2 * core, q)
-        at = rows_of(shard_of(q, t) + 1 - 2 * core, q)
         remote(wbuf.at[at], wbuf.at[at], twin_s.at[q, t], twin_r.at[q, t], twin).wait_recv()
 
-    own_rows = pl.ds(pl.multiple_of(me * depth, depth), depth)
-    own = pltpu.make_async_copy(w_ref, wbuf.at[own_rows], local_sem.at[0])
-    own.start()
-    own.wait()
+    def xt_wait(d, t):
+        at = other_rows(shard_of(2 * d, t) + 1 - 2 * core, d)
+        remote(wbuf.at[at], wbuf.at[at], xt_s.at[d, t], xt_r.at[d, t], twin).wait_recv()
+
+    def x_step(t):
+        for d in range(2):
+            x_copy(d, t, other_rows(shard_of(2 * d, t), d)).wait_recv()
+            xt_copy(d, t).start()
+
+    loads[0].wait()
+
+    def idx_copy(j, block):
+        return remote(idx_send, idx_all.at[block], idx_s.at[j], idx_r.at[j], lax.rem(me + j, n))
+
+    @pl.loop(1, n)
+    def _(j):
+        idx_copy(j, me).start()
+
     for q in (0, 2, 1, 3):
         ring_copy(q, 0).start()
     for q in range(4):
         twin_copy(q, 0).start()
-
-    def idx_copy(j, block):
-        return remote(idx_send, idx_all.at[block], idx_s.at[j], idx_r.at[j], lax.rem(me + j, n))
-
-    @pl.loop(1, n)
-    def _(j):
-        idx_copy(j, me).start()
-
+    for d in range(2):
+        xt_copy(d, 0).start()
     idx_own = pltpu.make_async_copy(idx_send, idx_all.at[me], local_sem.at[1])
     idx_own.start()
 
+    loads[1].wait()
+    loads[2].wait()
     row = lax.broadcasted_iota(jnp.int32, (rows, 1), 0)
     live = row < lens_ref[0]
     for s in range(1, seqs):
@@ -138,6 +184,7 @@
         dev = lax.rem(me + j, n)
         return remote(csend.at[dev], od.at[block], c_s.at[j], c_r.at[j], dev)
 
+    loads[3].wait()
     for s in range(seqs):
         od[me, pl.ds(s * rank, rank), :] = down_ref[own_idx_ref[s]]
 
@@ -153,6 +200,8 @@
             ring_wait(q, t)
             if not last:
                 ring_copy(q, t).start()
+            if q % 2:
+                x_send(q // 2, t).start()
             twin_copy(q, t).start()
 
     def column(shard, h):
@@ -179,6 +228,8 @@
     def twin_arrive(t):
         for q in range(4):
             twin_wait(q, t)
+        for d in range(2):
+            xt_wait(d, t)
 
     def d_copy(j, block):
         dev = lax.rem(me + j, n)
@@ -195,24 +246,29 @@
             d_copy(j, me).start()
 
     acc[...] = jnp.zeros_like(acc)
+    loads[4].wait()
+    per = n // 4
     forward(1, False)
-    d_range(1, n // 2)
-    d_term(me)
-    d_own = pltpu.make_async_copy(dsend.at[me], drecv.at[me], local_sem.at[2])
-    d_own.start()
+    d_range(1, per)
     forward(2, False)
-    d_range(n // 2, n)
+    x_step(1)
+    d_range(per, 2 * per)
     own_part(0, fwd)
     own_part(1, fwd)
     twin_arrive(0)
     twin_part(0, fwd)
+    forward(3, False)
+    x_step(2)
+    d_range(2 * per, 3 * per)
     own_part(2, fwd)
     twin_arrive(1)
     twin_part(1, fwd)
-    forward(3, False)
-    own_part(3, fwd)
-    twin_arrive(2)
-    twin_part(2, fwd)
+    forward(4, False)
+    x_step(3)
+    d_range(3 * per, n)
+    d_term(me)
+    d_own = pltpu.make_async_copy(dsend.at[me], drecv.at[me], local_sem.at[2])
+    d_own.start()
 
     @pl.loop(1, n)
     def _(j):
@@ -247,35 +303,45 @@
         fwd(shard, h)
         bwd(shard, h)
 
-    forward(4, False)
-
-    @pl.loop(0, 4)
+    @pl.loop(0, 3)
     def _(t):
         own_part(t, bwd)
 
-    @pl.loop(0, 3)
+    @pl.loop(0, 2)
     def _(t):
         twin_part(t, bwd)
 
     @pl.loop(4, chips - 1)
     def _(t):
-        twin_arrive(t - 1)
-        own_part(t, both)
-        twin_part(t - 1, both)
+        own_part(t - 1, both)
+        twin_arrive(t - 2)
+        twin_part(t - 2, both)
 
         @pl.when(t < chips - 2)
         def _():
             forward(t + 1, False)
 
-    forward(chips - 1, True)
+        @pl.when(t == chips - 2)
+        def _():
+            forward(chips - 1, True)
+
+        x_step(t)
+
+    own_part(chips - 2, both)
+    twin_arrive(chips - 3)
+    twin_part(chips - 3, both)
+    x_step(chips - 1)
     own_part(chips - 1, both)
     twin_arrive(chips - 2)
     twin_part(chips - 2, both)
     twin_arrive(chips - 1)
     twin_part(chips - 1, both)
+    store = pltpu.make_async_copy(tig_ref, tig_hbm, store_sem.at[0])
+    store.start()
     out = scale_ref[0] * acc[...] + adapter_scale * adapter_out
     proj_ref[...] = jnp.where(live, out, 0.0).astype(bf16)
 
+    store.wait()
     d_own.wait()
     u_own.wait()
 
@@ -293,6 +359,13 @@
     def _(t):
         for q in range(4):
             twin_copy(q, t).wait_send()
+        for d in range(2):
+            xt_copy(d, t).wait_send()
+
+    @pl.loop(1, chips)
+    def _(t):
+        for d in range(2):
+            x_send(d, t).wait_send()
 
     @pl.loop(0, chips - 1)
     def _(t):
@@ -300,13 +373,29 @@
             ring_copy(q, t).wait_send()
 
 
-def gather_adapters(idx_ref, d_ref, out_ref):
+def gather_adapters(idx_ref, d_ref, tig_ref, out_ref, tig_out, held, sems):
+    parts = sems.shape[1]
+    size = tig_ref.shape[0] // parts
+    loads, stores = [], []
+    for i in range(parts):
+        at = pl.ds(i * size, size)
+        loads.append(pltpu.make_async_copy(tig_ref.at[at], held.at[at], sems.at[0, i]))
+        stores.append(pltpu.make_async_copy(held.at[at], tig_out.at[at], sems.at[1, i]))
+    for load in loads:
+        load.start()
     out_ref[...] = jnp.zeros_like(out_ref)
+
+    for load, store in zip(loads, stores):
+        load.wait()
+        store.start()
 
     @pl.loop(0, d_ref.shape[0])
     def _(k):
         i = idx_ref[k]
         out_ref[i] = out_ref[i] + d_ref[k]
+
+    for store in stores:
+        store.wait()
 
 
 def local_ring(
@@ -343,9 +432,14 @@
             jax.ShapeDtypeStruct((n, sr, depth), f32),
             jax.ShapeDtypeStruct((n, cols, sr), f32),
         ),
-        in_specs=[smem, smem, smem, vmem, vmem, vmem, vmem, vmem],
-        out_specs=(vmem, vmem, hbm, hbm, hbm),
+        in_specs=[smem, smem, smem, hbm, hbm, hbm, hbm, hbm],
+        out_specs=(vmem, hbm, hbm, hbm, hbm),
         scratch_shapes=[
+            pltpu.VMEM((rows, width), bf16),
+            pltpu.VMEM((rows, out_width), bf16),
+            pltpu.VMEM((adapters, rank, depth), bf16),
+            pltpu.VMEM((adapters, rank, out_width), bf16),
+            pltpu.VMEM((rows, width), bf16),
             pltpu.VMEM((width, out_width), bf16),
             pltpu.VMEM((n, sr, depth), bf16),
             pltpu.VMEM((n, sr, depth), bf16),
@@ -361,9 +455,11 @@
             dma((n,)), dma((n,)), dma((n,)), dma((n,)),
             dma((n,)), dma((n,)), dma((n,)), dma((n,)),
             dma((4, chips)), dma((4, chips)), dma((4, chips)), dma((4, chips)),
+            dma((2, chips)), dma((2, chips)), dma((2, chips)), dma((2, chips)),
+            dma((5,)), dma((1,)),
         ],
         compiler_params=pltpu.CompilerParams(
-            collective_id=0, has_side_effects=True, vmem_limit_bytes=48 * 2**20
+            collective_id=0, has_side_effects=True, vmem_limit_bytes=60 * 2**20
         ),
         cost_estimate=pl.CostEstimate(
             flops=4 * rows * width * out_width, bytes_accessed=2 * rows * width * 2,
@@ -374,13 +470,17 @@
         frozen_weight, jnp.swapaxes(adapter_down_weight, 1, 2), adapter_up_weight,
     )
     every_index = idx_all[:, 0, :seqs].reshape(total)
-    down_grad = pl.pallas_call(
+    down_grad, tig = pl.pallas_call(
         gather_adapters,
-        out_shape=jax.ShapeDtypeStruct((adapters, rank, depth), f32),
-        in_specs=[smem, vmem],
-        out_specs=vmem,
-        compiler_params=pltpu.CompilerParams(vmem_limit_bytes=16 * 2**20),
-    )(every_index, drecv.reshape(total, rank, depth))
+        out_shape=(
+            jax.ShapeDtypeStruct((adapters, rank, depth), f32),
+            jax.ShapeDtypeStruct((rows, width), bf16),
+        ),
+        in_specs=[smem, vmem, hbm],
+        out_specs=(vmem, hbm),
+        scratch_shapes=[pltpu.VMEM((rows, width), bf16), dma((2, 8))],
+        compiler_params=pltpu.CompilerParams(vmem_limit_bytes=60 * 2**20),
+    )(every_index, drecv.reshape(total, rank, depth), tig)
     select = (every_index[None, :] == jnp.arange(adapters, dtype=jnp.int32)[:, None]).astype(f32)
     up_seq = jnp.transpose(urecv.reshape(n, cols, seqs, rank), (0, 2, 3, 1)).reshape(total, rank * cols)
     up_grad = (
@@ -487,7 +587,7 @@
         P(("groups", "dp")),
     )
     n = mesh.shape["dp"]
-    ring = n % 4 == 0 and n >= 12 and n <= 32
+    ring = n == 16 and mesh.shape["groups"] == 2
     return jax.shard_map(
         functools.partial(local_ring, n) if ring else local,
         mesh=mesh,

time: 116 us -> 102 us (0.88)
  local copies, waits for them, and re-layouts: 12.3 us -> 3.76 us
  Pallas kernels: 101 us -> 96.1 us
    unnamed x14 -> x5, local copies, waits for them, and re-layouts: 11.1 us -> 0.72 us
    pallas_call x1, Pallas kernels: 98.3 us -> 90 us  [local_ring(): pl.pallas_call(functools.partial(exchange, n, slot, rank), out_shape=(jax...]
    pallas_call x1, Pallas kernels: 2.25 us -> 6.13 us  [local_ring(): pl.pallas_call(gather_adapters, out_shape=(jax.ShapeDtypeStruct((adapters...]
where the time goes in v3:
time: 102 us; the launch traced here: 101 us
  Pallas kernels  96.1 us (94%)
  local copies, waits for them, and re-layouts  3.76 us (4%)
  between operations  1.34 us (1%)
    pallas_call x1, Pallas kernels, local_ring(): pl.pallas_call(functools.partial(exchange, n, slot, rank), out_shape=(jax...  90 us
    pallas_call x1, Pallas kernels, local_ring(): pl.pallas_call(gather_adapters, out_shape=(jax.ShapeDtypeStruct((adapters...  6.13 us

profile of v3, /device:TPU:5, one launch (start us, length us, event | category | flops | bytes accessed | tf_op | source)
XLA Modules:
  0.0 101.4 jit_solution(13072628259167066242)
XLA Ops:
  1.3 90.0 %shard_map.111 = (bf16[256,512]{1,0:T(8,128)(2,1)}, bf16[256,8192]{1,0:T(8,128)(2,1)}, s32[16,8,128]{2,1,0:T(8,128)}, f32[16,32,512]{2,1,0:T(8,128)}, f32[16,32,32]{2,1,0:T(8,128)}) custom-call(s32[2]{0:T(128)} %lens_ref.1, s32[2]{0:T(128)} %own_idx_ref.1, f32[1]{0:T(128)S(6)} %copy.16.scale_ref, bf16[256,8192]{1,0:T(8,128)(2,1)} %tok_hbm.1, ...), custom_call_target="tpu_custom_call" | custom-call | flops 4294967296 | bytes 8388608 | tf_op jit(solution)/shard_map/pallas_call | solution.py:426
  91.3 0.0 copy-start
  91.3 0.9 slice_reduce_fusion
  92.2 0.1 reshape_squeeze.3.idx_ref
  92.3 0.0 copy-start.1
  92.3 1.1 %copy.13 = f32[16,32,32]{1,2,0:T(8,128)S(1)} copy(f32[16,32,32]{2,1,0:T(8,128)} %get-tuple-element.17) | data formatting | bytes 131072 | tf_op jit(solution)/shard_map/pallas_call | solution.py:426
  93.4 0.1 reshape.23
  93.5 0.2 convolution_multiply_fusion
  93.7 0.8 copy.14
  94.6 0.0 copy-done.1
  94.6 6.1 %shard_map.112 = (f32[64,16,512]{2,1,0:T(8,128)}, bf16[256,8192]{1,0:T(8,128)(2,1)}) custom-call(s32[32]{0:T(128)} %copy-done.1, f32[32,16,512]{2,1,0:T(8,128)} %bitcast.11, bf16[256,8192]{1,0:T(8,128)(2,1)} %get-tuple-element.14.tig_ref), custom_call_target="tpu_custom_call" | custom-call | tf_op jit(solution)/shard_map/pallas_call | solution.py:473
  100.7 0.0 copy-done
  100.7 0.7 copy.17
Async XLA Ops:
  91.3 9.4 %copy-start = (bf16[256,512]{1,0:T(8,128)(2,1)S(1)}, bf16[256,512]{1,0:T(8,128)(2,1)}, u32[]{:S(2)}) copy-start(bf16[256,512]{1,0:T(8,128)(2,1)} %get-tuple-element.26) | copy-start | bytes 786436
  92.3 2.3 %copy-start.1 = (s32[32]{0:T(128)}, s32[32]{0:T(128)S(1)}, u32[]{:S(2)}) copy-start(s32[32]{0:T(128)S(1)} %reshape_squeeze.3.idx_ref) | copy-start | bytes 388

commit v4 on v3

--- a/solution.py
+++ b/solution.py
@@ -25,7 +25,7 @@
     seqs = rows // slot
     depth = w_ref.shape[0]
     half = depth // 2
-    shared, single = half * 3 // 8, half * 5 // 16
+    shared, single = half // 4, half * 3 // 8
     plane = lax.axis_index("groups")
     chips = n // 2
     side = chips // 2
@@ -170,6 +170,24 @@
     g = adapter_scale * lax.dot_general(mc, up2, NT, preferred_element_type=f32)
     g_ref[...] = jnp.where(diag, g, 0.0).astype(bf16)
 
+    def d_copy(j, block):
+        dev = lax.rem(me + j, n)
+        return remote(dsend.at[dev], drecv.at[block], d_s.at[j], d_r.at[j], dev)
+
+    def d_term(dev):
+        at = pl.ds(pl.multiple_of(dev * depth, depth), depth)
+        dsend[dev] = lax.dot_general(g_ref[...], tok_ref[:, at], TN, preferred_element_type=f32)
+
+    def d_range(first, last):
+        @pl.loop(first, last)
+        def _(j):
+            d_term(lax.rem(me + j, n))
+            d_copy(j, me).start()
+
+    per = n // 4
+    loads[4].wait()
+    d_range(1, per)
+
     idx_own.wait()
 
     @pl.loop(1, n)
@@ -231,41 +249,24 @@
         for d in range(2):
             xt_wait(d, t)
 
-    def d_copy(j, block):
-        dev = lax.rem(me + j, n)
-        return remote(dsend.at[dev], drecv.at[block], d_s.at[j], d_r.at[j], dev)
-
-    def d_term(dev):
-        at = pl.ds(pl.multiple_of(dev * depth, depth), depth)
-        dsend[dev] = lax.dot_general(g_ref[...], tok_ref[:, at], TN, preferred_element_type=f32)
-
-    def d_range(first, last):
-        @pl.loop(first, last)
-        def _(j):
-            d_term(lax.rem(me + j, n))
-            d_copy(j, me).start()
-
     acc[...] = jnp.zeros_like(acc)
-    loads[4].wait()
-    per = n // 4
     forward(1, False)
-    d_range(1, per)
+    d_range(per, 2 * per)
     forward(2, False)
     x_step(1)
-    d_range(per, 2 * per)
+    d_range(2 * per, 3 * per)
     own_part(0, fwd)
     own_part(1, fwd)
     twin_arrive(0)
     twin_part(0, fwd)
     forward(3, False)
     x_step(2)
-    d_range(2 * per, 3 * per)
+    d_range(3 * per, n)
     own_part(2, fwd)
     twin_arrive(1)
     twin_part(1, fwd)
     forward(4, False)
     x_step(3)
-    d_range(3 * per, n)
     d_term(me)
     d_own = pltpu.make_async_copy(dsend.at[me], drecv.at[me], local_sem.at[2])
     d_own.start()

time: 102 us -> 99.8 us (0.978)
  Pallas kernels: 96.1 us -> 93.6 us
    pallas_call x1, Pallas kernels: 90 us -> 87.5 us  [local_ring(): pl.pallas_call(functools.partial(exchange, n, slot, rank), out_shape=(jax...]
where the time goes in v4:
time: 99.8 us; the launch traced here: 98.9 us
  Pallas kernels  93.6 us (94%)
  local copies, waits for them, and re-layouts  3.76 us (4%)
  between operations  1.34 us (1%)
    pallas_call x1, Pallas kernels, local_ring(): pl.pallas_call(functools.partial(exchange, n, slot, rank), out_shape=(jax...  87.5 us
    pallas_call x1, Pallas kernels, local_ring(): pl.pallas_call(gather_adapters, out_shape=(jax.ShapeDtypeStruct((adapters...  6.13 us

profile of v4, /device:TPU:5, one launch (start us, length us, event | category | flops | bytes accessed | tf_op | source)
XLA Modules:
  0.0 98.9 jit_solution(7905395541675399098)
XLA Ops:
  1.3 87.5 %shard_map.111 = (bf16[256,512]{1,0:T(8,128)(2,1)}, bf16[256,8192]{1,0:T(8,128)(2,1)}, s32[16,8,128]{2,1,0:T(8,128)}, f32[16,32,512]{2,1,0:T(8,128)}, f32[16,32,32]{2,1,0:T(8,128)}) custom-call(s32[2]{0:T(128)} %lens_ref.1, s32[2]{0:T(128)} %own_idx_ref.1, f32[1]{0:T(128)S(6)} %copy.16.scale_ref, bf16[256,8192]{1,0:T(8,128)(2,1)} %tok_hbm.1, ...), custom_call_target="tpu_custom_call" | custom-call | flops 4294967296 | bytes 8388608 | tf_op jit(solution)/shard_map/pallas_call | solution.py:427
  88.8 0.0 copy-start
  88.8 0.9 slice_reduce_fusion
  89.7 0.1 reshape_squeeze.3.idx_ref
  89.8 0.0 copy-start.1
  89.8 1.1 %copy.13 = f32[16,32,32]{1,2,0:T(8,128)S(1)} copy(f32[16,32,32]{2,1,0:T(8,128)} %get-tuple-element.17) | data formatting | bytes 131072 | tf_op jit(solution)/shard_map/pallas_call | solution.py:427
  90.9 0.1 reshape.23
  91.0 0.2 convolution_multiply_fusion
  91.2 0.8 copy.14
  92.1 0.0 copy-done.1
  92.1 6.1 %shard_map.112 = (f32[64,16,512]{2,1,0:T(8,128)}, bf16[256,8192]{1,0:T(8,128)(2,1)}) custom-call(s32[32]{0:T(128)} %copy-done.1, f32[32,16,512]{2,1,0:T(8,128)} %bitcast.11, bf16[256,8192]{1,0:T(8,128)(2,1)} %get-tuple-element.14.tig_ref), custom_call_target="tpu_custom_call" | custom-call | tf_op jit(solution)/shard_map/pallas_call | solution.py:474
  98.2 0.0 copy-done
  98.2 0.7 copy.17
Async XLA Ops:
  88.8 9.4 %copy-start = (bf16[256,512]{1,0:T(8,128)(2,1)S(1)}, bf16[256,512]{1,0:T(8,128)(2,1)}, u32[]{:S(2)}) copy-start(bf16[256,512]{1,0:T(8,128)(2,1)} %get-tuple-element.26) | copy-start | bytes 786436
  89.8 2.3 %copy-start.1 = (s32[32]{0:T(128)}, s32[32]{0:T(128)S(1)}, u32[]{:S(2)}) copy-start(s32[32]{0:T(128)S(1)} %reshape_squeeze.3.idx_ref) | copy-start | bytes 388
